TPU v7x, 128 devices: a whole 4x4x4 slice. The times are simulated.
128 devices in a mesh: seq: 32 (over z, y, core), head: 4 (over x).
Axes of the slice: x: 4, y: 4, z: 4, core: 2. Of those that a mesh axis runs over, the one named last changes fastest.
Arguments:
- tokens: bfloat16 [8192, 2048], P('seq'), may hold values from -6 to 6
- turn_ids: int32 [8192], P('seq'), may hold values from 1 to 8, as said below
- q_weight: bfloat16 [2048, 2048], P(None, 'head'), may hold values from -0.125 to 0.125
- k_weight: bfloat16 [2048, 4096], P(None, 'head'), may hold values from -0.125 to 0.125
- v_weight: bfloat16 [2048, 4096], P(None, 'head'), may hold values from -0.125 to 0.125
- beta_weight: bfloat16 [2048, 32], P(None, 'head'), may hold values from -0.0625 to 0.0625
- beta_bias: float32 [32], P('head'), may hold values from -6 to 6
- norm_gain: float32 [2048], P('head'), may hold values from 0.1 to 1.9
- out_weight: bfloat16 [2048, 2048], P('head'), may hold values from -0.125 to 0.125
Outputs:
- mixed: bfloat16 [8192, 2048], P(('seq', 'head'))
Inputs may be any that keep to these rules, and one draw needn't show every extreme that they name: `turn_ids`: turn numbers never fall along the sequence; every turn holds 1 to 2048 tokens and one holds exactly 2048.
All inputs are finite; a program needn't handle non-finite values.
Results may differ from a plain program's by a relative error of at most 0.018.
Values may be sent and summed in bfloat16 or wider, within the bound.
A program may use at most 128 MiB of HBM per device.

v0:
```python
import jax
import jax.numpy as jnp
from jax import lax
from jax.sharding import PartitionSpec as P

DK = 128
DV = 128
SPAN = 64


key_eps = 1e-06
norm_eps = 1e-05


def shifted(block, axis, distance):
    devices = range(lax.axis_size(axis))
    route = [(i - distance, i) for i in devices if i - distance in devices]
    return lax.ppermute(block, axis, route)


def prefix(array, axis, combine, identity):
    size, place = (lax.axis_size(axis), lax.axis_index(axis))
    everything = jax.tree.map(
        lambda part, kind: lax.all_gather(part.astype(kind), axis),
        array,
        (jnp.bfloat16, jnp.bfloat16),
    )
    start = jax.tree.map(
        lambda part, zero: jnp.broadcast_to(jnp.asarray(zero, part.dtype), part.shape),
        array,
        identity,
    )

    def turn(k, before):
        reached = k < place
        new = combine(
            before, jax.tree.map(lambda part, own: part[k].astype(own.dtype), everything, array)
        )
        return jax.tree.map(lambda a, b: jnp.where(reached, a, b), new, before)

    return lax.fori_loop(0, size, turn, start)


def normalize(vectors):
    return vectors * lax.rsqrt(jnp.sum(vectors * vectors, axis=-1, keepdims=True) + key_eps)


def project(tokens, q_weight, k_weight, v_weight, beta_weight, beta_bias):
    rows = tokens.shape[0]
    queries = jnp.dot(tokens, q_weight, preferred_element_type=jnp.float32).reshape(rows, -1, DK)
    keys = jnp.dot(tokens, k_weight, preferred_element_type=jnp.float32).reshape(rows, -1, 2, DK)
    values = jnp.dot(tokens, v_weight, preferred_element_type=jnp.float32).reshape(rows, -1, 2, DV)
    logits = jnp.dot(tokens, beta_weight, preferred_element_type=jnp.float32) + beta_bias
    betas = (2.0 * jax.nn.sigmoid(logits)).reshape(rows, -1, 2)
    return (normalize(queries), normalize(keys), values, betas)


def blocks(queries, keys, values, betas, turn_ids):
    rows, heads = (queries.shape[0], queries.shape[1])
    count = rows // SPAN
    query_blocks = queries.transpose(1, 0, 2).reshape(heads, count, SPAN, DK)
    key_blocks = keys.transpose(1, 0, 2, 3).reshape(heads, count, 2 * SPAN, DK)
    value_blocks = values.transpose(1, 0, 2, 3).reshape(heads, count, 2 * SPAN, DV)
    beta_blocks = betas.transpose(1, 0, 2).reshape(heads, count, 2 * SPAN)
    turn_blocks = turn_ids.reshape(count, SPAN)
    return (query_blocks, key_blocks, value_blocks, beta_blocks, turn_blocks)


def span_terms(queries, keys, values, betas, turns, before):
    highest = lax.Precision.HIGHEST
    refl_count = keys.shape[0]
    tok_count = queries.shape[0]
    turn_refl = jnp.repeat(turns, 2)
    carried = (turn_refl == before).astype(jnp.float32)
    same_turn = turn_refl[:, None] == turn_refl[None, :]
    key_gram = jnp.dot(keys, keys.T, precision=highest)
    lower = jnp.tril(jnp.where(same_turn, key_gram, 0.0), -1)
    system = jnp.eye(refl_count, dtype=jnp.float32) + betas[:, None] * lower
    solved = jax.scipy.linalg.solve_triangular(system, jnp.diag(betas), lower=True)
    solved_keys = jnp.dot(solved, carried[:, None] * keys, precision=highest)
    solved_values = jnp.dot(solved, values, precision=highest)
    last_turn = (turn_refl == turn_refl[-1]).astype(jnp.float32)
    lift = carried[-1] * jnp.eye(DK, dtype=jnp.float32) - jnp.dot(
        keys.T, last_turn[:, None] * solved_keys, precision=highest
    )
    write = jnp.dot(keys.T, last_turn[:, None] * solved_values, precision=highest)
    scores = jnp.dot(queries, keys.T, precision=highest)
    visible = (jnp.arange(refl_count)[None, :] // 2 <= jnp.arange(tok_count)[:, None]) & (
        turns[:, None] == turn_refl[None, :]
    )
    masked = jnp.where(visible, scores, 0.0)
    local_out = jnp.dot(masked, solved_values, precision=highest)
    query_live = (turns == before).astype(jnp.float32)
    through = query_live[:, None] * queries - jnp.dot(masked, solved_keys, precision=highest)
    return (lift, write, local_out, through)


def finish(outputs, norm_gain):
    scaled = outputs * lax.rsqrt(jnp.mean(outputs * outputs, axis=-1, keepdims=True) + norm_eps)
    return (scaled.reshape(outputs.shape[0], -1) * norm_gain).astype(jnp.bfloat16)


def matmul_heads(left, right):
    return jnp.einsum("hij,hjk->hik", left, right, precision=lax.Precision.HIGHEST)


def combine(earlier, later):
    return (matmul_heads(later[0], earlier[0]), matmul_heads(later[0], earlier[1]) + later[1])


def body(
    tokens, turn_ids, q_weight, k_weight, v_weight, beta_weight, beta_bias, norm_gain, out_weight
):
    highest = lax.Precision.HIGHEST
    tok_rows = tokens.shape[0]
    queries, keys, values, betas = project(
        tokens, q_weight, k_weight, v_weight, beta_weight, beta_bias
    )
    previous = shifted(turn_ids[-1:], "seq", 1)
    before = jnp.concatenate([previous, turn_ids[:-1]])[::SPAN]
    query_blocks, key_blocks, value_blocks, beta_blocks, turn_blocks = blocks(
        queries, keys, values, betas, turn_ids
    )
    lift, write, local_out, through = jax.vmap(
        jax.vmap(span_terms), in_axes=(0, 0, 0, 0, None, None)
    )(query_blocks, key_blocks, value_blocks, beta_blocks, turn_blocks, before)
    heads_here = lift.shape[0]
    identity_lift = jnp.broadcast_to(jnp.eye(DK, dtype=jnp.float32), (heads_here, DK, DK))
    empty_state = jnp.zeros((heads_here, DK, DV), jnp.float32)

    def compose(carry, items):
        return (combine(carry, items), carry)

    device_pair, prefix_pair = lax.scan(
        compose, (identity_lift, empty_state), (jnp.moveaxis(lift, 1, 0), jnp.moveaxis(write, 1, 0))
    )
    dev_lift, dev_write = device_pair
    pre_lift = jnp.moveaxis(prefix_pair[0], 0, 1)
    pre_write = jnp.moveaxis(prefix_pair[1], 0, 1)
    incoming = prefix((dev_lift, dev_write), "seq", combine, (identity_lift, empty_state))[1]
    states = jnp.einsum("hcij,hjv->hciv", pre_lift, incoming, precision=highest) + pre_write
    results = local_out + jnp.einsum("hcrk,hckv->hcrv", through, states, precision=highest)
    outputs = results.transpose(1, 2, 0, 3).reshape(tok_rows, heads_here, DV)
    hidden = finish(outputs, norm_gain)
    return lax.psum_scatter(
        jnp.dot(hidden, out_weight, preferred_element_type=jnp.float32).astype(jnp.bfloat16),
        "head",
        scatter_dimension=0,
        tiled=True,
    )


def solution(mesh):
    return jax.shard_map(
        body,
        mesh=mesh,
        in_specs=(
            P("seq", None),
            P("seq"),
            P(None, "head"),
            P(None, "head"),
            P(None, "head"),
            P(None, "head"),
            P("head"),
            P("head"),
            P("head", None),
        ),
        out_specs=P(("seq", "head"), None),
        check_vma=False,
    )
```

profile of v0, /device:TPU:1, one launch (start us, length us, event | category | flops | bytes accessed | tf_op | source)
XLA Modules:
  0.0 420.5 jit_solution(17820848288408133699)
XLA Ops:
  8.0 4.6 %collective-permute-start = (s32[1]{0:T(128)}, s32[1]{0:T(128)}, u32[]{:S(2)}, u32[]{:S(2)}) collective-permute-start(s32[1]{0:T(128)} %slice.21), channel_id=1, source_target_pairs={{0,4},{4,8},{8,12},{12,16},{16,20},{20,24},{24,28},{28,32},{32,36}... | collective-permute-start | bytes 20 | tf_op jit(solution)/shard_map/ppermute | solution.py:18
  14.2 1.6 fusion.30
  18.3 4.8 %fusion.54 = f32[256,1024]{1,0:T(8,128)} fusion(bf16[256,2048]{1,0:T(8,128)(2,1)} %param.13, bf16[2048,1024]{1,0:T(8,128)(2,1)} %param.16), kind=kOutput, calls=%fused_computation.93 | convolution fusion | flops 1073741824 | bytes 6291456 | tf_op jit(solution)/shard_map/dot_general | solution.py:51
  23.1 2.1 reshape.219
  25.2 2.4 multiply_reduce_fusion
  30.0 3.0 copy_multiply_fusion
  33.0 3.4 fusion.24
  36.4 158.6 %custom-call.4 = f32[4,4,1,128,128]{3,4,2,1,0:T(8,128)} custom-call(f32[4,4,1,128,128]{4,3,2,1,0:T(8,128)} %fusion.24), custom_call_target="InvertDiagBlocksLowerTriangular" | custom-call | tf_op jit(solution)/shard_map/vmap(vmap(jit(_solve_triangular)))/triangular_solve | solution.py:79
  195.0 4.8 %fusion.55 = f32[256,1024]{1,0:T(8,128)} fusion(bf16[256,2048]{1,0:T(8,128)(2,1)} %param.13, bf16[2048,1024]{1,0:T(8,128)(2,1)} %param.17), kind=kOutput, calls=%fused_computation.94 | convolution fusion | flops 1073741824 | bytes 6291456 | tf_op jit(solution)/shard_map/dot_general | solution.py:52
  199.8 3.1 reshape.222
  204.5 3.4 fusion.32
  210.1 2.9 convolution_bitcast_fusion
  214.0 2.5 fusion.37
  217.5 3.0 fusion.19
  222.6 21.3 %while.31 = (s32[]{:T(128)}, f32[4,128,128]{2,1,0:T(8,128)S(1)}, f32[4,128,128]{2,1,0:T(8,128)}, f32[4,4,128,128]{3,2,1,0:T(8,128)}, f32[4,4,128,128]{3,2,1,0:T(...) while((s32[]{:T(128)}, f32[4,128,128]{2,1,0:T(8,128)S(1)}, ...), condition=%wide.region_3.4_spmd.clone, body=%wide.region_2.3_spmd.clone.sunk | while | flops 201523200 | bytes 3933815 | solution.py:134
  224.5 2.1 convolution_add_fusion.6
  229.8 2.1 convolution_add_fusion.6
  235.1 2.1 convolution_add_fusion.6
  240.4 2.1 convolution_add_fusion.6
  244.7 1.6 convert_element_type.68
  246.4 3.5 fusion.53
  249.8 2.0 reshape.217
  255.0 2.1 convolution_select_fusion.1
  257.1 1.9 fusion.57
  259.1 1.9 convolution_subtract_fusion.1
  261.0 32.2 %all-gather.5.cloned.1.call-done = bf16[128,128,128]{2,1,0:T(8,128)(2,1)} async-done(((bf16[4,128,128]{2,1,0:T(8,128)(2,1)}), bf16[128,128,128]{2,1,0:T(8,128)(2,1)}) %all-gather.5.cloned.1.call-update) | async-done | bytes 4194320 | tf_op jit(solution)/shard_map/all_gather | solution.py:24
  293.2 48.0 %all-gather.7.cloned.1.call-done = bf16[128,128,128]{2,1,0:T(8,128)(2,1)} async-done(((bf16[4,128,128]{2,1,0:T(8,128)(2,1)}), bf16[128,128,128]{2,1,0:T(8,128)(2,1)}) %all-gather.7.cloned.1.call-update) | async-done | bytes 4194320 | tf_op jit(solution)/shard_map/all_gather | solution.py:24
  341.2 42.1 %while.32 = (s32[]{:T(128)}, f32[4,128,128]{2,1,0:T(8,128)S(1)}, s32[]{:T(128)}, bf16[32,4,128,128]{3,2,1,0:T(8,128)(2,1)}, bf16[32,4,128,128]{3,2,1,0:T(8,128)(2,1)}, /*index=5*/s32[]{:T(128)}, s32[]{:T(128)}) while((s32[]{:T(128)}, f32[4,128,128]{2,1,0:T(8,128)S(1)}, s32[]{:T(128)}, bf16[32,4,128,128]{3,2,1,0:T(8,128)(2,1)}, ...), condition=%wide.region_5.6_spmd.clone, body=%wide.region_4.5_spmd.clone.sunk | while | flops 100990976 | bytes 1575527 | solution.py:41
  383.3 2.6 convolution_add_fusion.2
  385.9 3.1 multiply_reduce_fusion.1
  390.9 1.7 convolution_convert_fusion
  392.7 21.3 %reduce-scatter.2.cloned.1.call-done = bf16[64,2048]{1,0:T(8,128)(2,1)} async-done(((bf16[256,2048]{1,0:T(8,128)(2,1)}), bf16[64,2048]{1,0:T(8,128)(2,1)}) %reduce-scatter.2.cloned.1.call-update) | async-done | bytes 262160 | tf_op jit(solution)/shard_map/reduce_scatter | solution.py:145
  (159 shorter events, 75.2 us)
Async XLA Ops:
  6.5 384.4 %copy-start = (bf16[512,2048]{1,0:T(8,128)(2,1)S(1)}, bf16[512,2048]{1,0:T(8,128)(2,1)}, u32[]{:S(2)}) copy-start(bf16[512,2048]{1,0:T(8,128)(2,1)} %param.21) | copy-start | bytes 6291460
  6.5 286.7 %all-gather.5.cloned.1.call-start = ((), (), s32[]{:S(2)}) async-start(), calls=%async_computation.2 | async-start | bytes 4325376 | tf_op jit(solution)/shard_map/all_gather | solution.py:24
  8.0 205.0 %collective-permute-start = (s32[1]{0:T(128)}, s32[1]{0:T(128)}, u32[]{:S(2)}, u32[]{:S(2)}) collective-permute-start(s32[1]{0:T(128)} %slice.21), channel_id=1, source_target_pairs={{0,4},{4,8},{8,12},{12,16},{16,20},{20,24},{24,28},{28,32},{32,36}... | collective-permute-start | bytes 20 | tf_op jit(solution)/shard_map/ppermute | solution.py:18
  23.1 9.9 %copy-start.7 = (pred[4,128,128]{2,1,0:T(8,128)(4,1)S(1)}, pred[4,128,128]{2,1,0:T(8,128)(4,1)}, u32[]{:S(2)}) copy-start(pred[4,128,128]{2,1,0:T(8,128)(4,1)} %broadcast_compare_fusion) | copy-start | bytes 196612
  23.1 9.9 %copy-start.9 = (pred[128,128]{1,0:T(8,128)(4,1)S(1)}, pred[128,128]{1,0:T(8,128)(4,1)}, u32[]{:S(2)}) copy-start(pred[128,128]{1,0:T(8,128)(4,1)} %get-tuple-element.249) | copy-start | bytes 49156
  23.1 9.9 %copy-start.10 = (pred[128,128]{1,0:T(8,128)(4,1)S(1)}, pred[128,128]{1,0:T(8,128)(4,1)}, u32[]{:S(2)}) copy-start(pred[128,128]{1,0:T(8,128)(4,1)} %get-tuple-element.250) | copy-start | bytes 49156
  25.2 3.7 copy-start.6
  195.0 9.4 %copy-start.8 = (pred[128,128]{1,0:T(8,128)(4,1)S(1)}, pred[128,128]{1,0:T(8,128)(4,1)}, u32[]{:S(2)}) copy-start(pred[128,128]{1,0:T(8,128)(4,1)} %iota_compare_fusion.1) | copy-start | bytes 49156
  202.9 7.2 %copy-start.11 = (f32[4,128]{1,0:T(4,128)S(1)}, f32[4,128]{1,0:T(4,128)}, u32[]{:S(2)}) copy-start(f32[4,128]{1,0:T(4,128)} %compare_convert_fusion.1) | copy-start | bytes 6148
  204.5 8.6 %copy-start.12 = (s32[256]{0:T(256)S(1)}, s32[256]{0:T(256)}, u32[]{:S(2)}) copy-start(s32[256]{0:T(256)} %param.14) | copy-start | bytes 3076
  207.8 5.2 %copy-start.5 = (f32[4,4,128,128]{3,2,1,0:T(8,128)}, f32[4,4,128,128]{3,2,1,0:T(8,128)S(1)}, u32[]{:S(2)}) copy-start(f32[4,4,128,128]{3,2,1,0:T(8,128)S(1)} %fusion.32) | copy-start | bytes 3145732
  209.0 1.1 copy-start.1
  216.5 1.0 copy-start.3
  244.6 96.6 %all-gather.7.cloned.1.call-start = ((), (), s32[]{:S(2)}) async-start(), calls=%async_computation.3 | async-start | bytes 4325376 | tf_op jit(solution)/shard_map/all_gather | solution.py:24
  246.3 167.6 %reduce-scatter.2.cloned.1.call-start = ((), (), s32[]{:S(2)}) async-start(), calls=%async_computation.1 | async-start | bytes 1310720 | tf_op jit(solution)/shard_map/reduce_scatter | solution.py:145
  251.8 5.3 %copy-start.2 = (f32[4,4,128,128]{3,2,1,0:T(8,128)S(1)}, f32[4,4,128,128]{3,2,1,0:T(8,128)}, u32[]{:S(2)}) copy-start(f32[4,4,128,128]{3,2,1,0:T(8,128)} %copy-done.1) | copy-start | bytes 3145732
  251.8 7.3 %copy-start.4 = (f32[4,4,128,128]{3,2,1,0:T(8,128)S(1)}, f32[4,4,128,128]{3,2,1,0:T(8,128)}, u32[]{:S(2)}) copy-start(f32[4,4,128,128]{3,2,1,0:T(8,128)} %copy-done.3) | copy-start | bytes 3145732
  383.3 7.6 %copy-start.13 = (f32[512]{0:T(512)S(1)}, f32[512]{0:T(512)}, u32[]{:S(2)}) copy-start(f32[512]{0:T(512)} %param.20) | copy-start | bytes 6148
Sparse Core Ops, SparseCore 0:
  244.7 48.4 all-gather.4
  295.5 45.6 all-gather.6
  392.8 21.1 reduce-scatter.1
where the time goes:
time: 423 us; the launch traced here: 420 us
  other arithmetic  176 us (42%)
  waiting for transfers between devices  102 us (24%)
  matrix products  98.4 us (23%)
  local copies, waits for them, and re-layouts  24.6 us (6%)
  between operations  13.5 us (3%)
  starting transfers between devices  4.67 us (1%)
    another operation x1, other arithmetic, span_terms(): jax.scipy.linalg.solve_triangular(system, jnp.diag(betas), lower=True)  159 us
    all_gather x2, waiting for transfers between devices, prefix(): lax.all_gather(part.astype(kind), axis)  80.2 us
    dot_general x40, matrix products, matmul_heads(): jnp.einsum('hij,hjk->hik', left, right, precision=lax.Precision.HIGHEST)  54.2 us
    reduce_scatter x1, waiting for transfers between devices, body(): lax.psum_scatter(jnp.dot(hidden, out_weight, preferred_element_type=jnp.f...  21.3 us
  transfers between devices with their start and end apart: 4, of which 3 were waited for; matrix products, arithmetic and copies ran while one was open for 51% of the time, Pallas kernels for 0%

commit v1 on v0

v1 whole, which is shorter than its diff:
```python
import functools

import jax
import jax.numpy as jnp
from jax import lax
from jax.experimental import pallas as pl
from jax.experimental.pallas import tpu as pltpu
from jax.sharding import PartitionSpec as P

F32, BF16 = jnp.float32, jnp.bfloat16
MESH = pl.DeviceIdType.MESH
DK = 128
BLK = 128
REFL = 2 * BLK
NB = 4
HERE = 2
key_eps = 1e-06
norm_eps = 1e-05

NN = (((1,), (0,)), ((), ()))
NT = (((1,), (1,)), ((), ()))


def dot(a, b, dims=NN):
    return lax.dot_general(a, b, dims, preferred_element_type=F32)


def halves(a):
    hi = a.astype(BF16)
    return hi, (a - hi.astype(F32)).astype(BF16)


def mm1(a, b, dims=NN):
    return dot(a.astype(BF16), b.astype(BF16), dims)


def mm3(a, b, dims=NN):
    ah, al = halves(a)
    bh, bl = halves(b)
    return dot(ah, bh, dims) + (dot(ah, bl, dims) + dot(al, bh, dims))


def iota(shape, axis):
    return lax.broadcasted_iota(jnp.int32, shape, axis)


def interleave(a, b):
    rows = a.shape[0]
    a = a.reshape(rows // 8, 1, 8, a.shape[1])
    b = b.reshape(rows // 8, 1, 8, b.shape[3] if b.ndim == 4 else b.shape[1])
    return jnp.concatenate([a, b], axis=1).reshape(2 * rows, a.shape[3])


def token_of(r):
    return (r // 16) * 8 + r % 8


def time_of(r):
    return token_of(r) * 2 + (r // 8) % 2


def normalize(v):
    return v * lax.rsqrt(jnp.sum(v * v, axis=-1, keepdims=True) + key_eps)


def kernel(
    tok, ids, qw, kw, vw, bw, bb, gain, ow,
    out,
    x_s, wk_s, wv_s, wq_s, bw_s, wo_s, ids_s, prev_s,
    k_s, v_s, q_s, beta_s, mask_s, vis_s, tid_s, edge_s, spread_s,
    cs_s, bc_s, xs_s, u_s, kt_s, pre_s, thr_s,
    send_s, recv_s, wrecv_s, hid_s, hid2_s, rs_s, rr_s,
    lsem, tsem, isem, esend, erecv, hsem, rsend, rrecv,
):
    seq = lax.axis_index("seq")
    head = lax.axis_index("head")
    nseq = lax.axis_size("seq")
    nhead = lax.axis_size("head")
    chips = nseq // 2
    chip, core = seq // 2, lax.rem(seq, 2)
    other = 1 - core

    def at(step, which):
        return (lax.rem(chip + step + chips, chips) * 2 + which, head)

    def along(step):
        return (seq, lax.rem(head + step + nhead, nhead))

    own_rows = pl.ds(pl.multiple_of(core * 256, 256), 256)
    col = lambda size, at_: pl.ds(pl.multiple_of(core * (2 * size) + at_, 128), size)
    local = [
        pltpu.make_async_copy(tok, x_s.at[own_rows], lsem.at[0]),
        pltpu.make_async_copy(ids, ids_s.at[core], lsem.at[1]),
        pltpu.make_async_copy(kw.at[:, pl.ds(pl.multiple_of(core * 512, 256), 256)], wk_s.at[0], lsem.at[2]),
        pltpu.make_async_copy(kw.at[:, pl.ds(pl.multiple_of(core * 512 + 256, 256), 256)], wk_s.at[1], lsem.at[3]),
        pltpu.make_async_copy(bw, bw_s, lsem.at[4]),
        pltpu.make_async_copy(vw.at[:, pl.ds(pl.multiple_of(core * 512, 256), 256)], wv_s.at[0], lsem.at[5]),
        pltpu.make_async_copy(vw.at[:, pl.ds(pl.multiple_of(core * 512 + 256, 256), 256)], wv_s.at[1], lsem.at[6]),
        pltpu.make_async_copy(qw.at[:, pl.ds(pl.multiple_of(core * 256, 256), 256)], wq_s, lsem.at[7]),
        pltpu.make_async_copy(ow, wo_s, lsem.at[8]),
    ]
    for c in local:
        c.start()

    barrier = pltpu.get_barrier_semaphore()
    peers = [at(0, other)]
    for step in (1, 2, 3, 4, -1, -2, -3, -4):
        peers.append(at(step, core))
    for step in (1, -1):
        peers.append(at(step, other))
        peers.append(along(step))
    for peer in peers:
        pl.semaphore_signal(barrier, inc=1, device_id=peer, device_id_type=MESH)
    pl.semaphore_wait(barrier, len(peers))

    def remote(src, dst, ssem, rsem, peer):
        return pltpu.make_async_remote_copy(
            src_ref=src, dst_ref=dst, send_sem=ssem, recv_sem=rsem, device_id=peer, device_id_type=MESH
        )

    swap_ids = remote(ids, ids_s.at[core], isem.at[0], isem.at[1], at(0, other))
    swap_ids.start()
    swap_tok = remote(tok, x_s.at[own_rows], tsem.at[0], tsem.at[1], at(0, other))
    swap_tok.start()
    next_same = remote(ids, prev_s.at[core], isem.at[2], isem.at[3], at(1, core))
    next_same.start()
    next_other = remote(ids, prev_s.at[core], isem.at[4], isem.at[5], at(1, other))
    next_other.start()

    sr, sc = iota((128, 2048), 0), iota((128, 2048), 1)
    spread_s[...] = ((sr // 16 == (sc % 128) // 16) & (sr % 16 == sc // 128)).astype(F32).astype(BF16)

    def project(rows):
        x = x_s[rows, :]
        for h in range(HERE):
            k_s[h, rows, :] = dot(x, wk_s[h])
        for h in range(HERE):
            v_s[h, rows, :] = dot(x, wv_s[h])
        q_s[rows, :] = dot(x, wq_s[...])
        logits = dot(x, bw_s[...]) + bb[...]
        beta_s[rows, :] = 2.0 * jax.nn.sigmoid(logits)

    for c in local[:8]:
        c.wait()
    project(own_rows)
    swap_tok.wait()
    project(pl.ds(pl.multiple_of(other * 256, 256), 256))

    swap_ids.wait()
    next_same.wait()
    next_other.wait()
    rr_, cc_ = iota((REFL, REFL), 0), iota((REFL, REFL), 1)
    earlier = time_of(rr_) > time_of(cc_)
    seen = token_of(iota((BLK, REFL), 1)) <= iota((BLK, REFL), 0)
    for b in range(NB):
        row = ids_s[b // 2, pl.ds(b % 2, 1), :].astype(F32)
        if b == 0:
            before = jnp.max(prev_s[1, pl.ds(1, 1), :].astype(F32), axis=1, keepdims=True)
            before = jnp.where(chip == 0, -1.0, before)
        else:
            before = jnp.max(ids_s[(b - 1) // 2, pl.ds((b - 1) % 2, 1), :].astype(F32), axis=1, keepdims=True)
        last = jnp.max(row, axis=1, keepdims=True)
        tcol = jnp.transpose(jnp.broadcast_to(row, (BLK, BLK)))
        rcol = interleave(tcol, tcol)
        rrow = jnp.transpose(rcol)
        mask_s[b] = jnp.where(
            earlier & (jnp.concatenate([rcol, rcol], axis=1) == jnp.concatenate([rrow, rrow], axis=0)), 1.0, 0.0
        )
        vis_s[b] = jnp.where(seen & (jnp.concatenate([tcol, tcol], axis=1) == rrow), 1.0, 0.0)
        tid_s[b] = tcol
        edge_s[b, 0] = jnp.broadcast_to(before, (BLK, 128))
        edge_s[b, 1] = jnp.broadcast_to(last, (BLK, 128))

    r128, c128 = iota((128, 128), 0), iota((128, 128), 1)
    eye = (r128 == c128).astype(F32)

    def level(t, a, size):
        odd = jnp.where(((r128 // (2 * size)) == (c128 // (2 * size))) & ((r128 // size) % 2 == 1) & ((c128 // size) % 2 == 0), a, 0.0)
        pick = lambda m: jnp.concatenate([m[i * size:(i + 1) * size] for i in range(1, 128 // size, 2)], axis=0)
        low = mm3(pick(odd), t)
        zero = jnp.zeros((size, 128), F32)
        full = jnp.concatenate(
            [piece for i in range(64 // size) for piece in (zero, low[i * size:(i + 1) * size])], axis=0
        )
        new = pick(t) - mm3(pick(t), full)
        return jnp.concatenate(
            [piece for i in range(64 // size) for piece in (t[2 * i * size:(2 * i + 1) * size], new[i * size:(i + 1) * size])],
            axis=0,
        )

    def maps(h, carry):
        betas = beta_s[...]
        lane = iota(betas.shape, 1)
        b0 = jnp.sum(jnp.where(lane == core * 4 + h * 2, betas, 0.0), axis=1, keepdims=True)
        b1 = jnp.sum(jnp.where(lane == core * 4 + h * 2 + 1, betas, 0.0), axis=1, keepdims=True)
        systems, rhs, kts = [], [], []
        for b in range(NB):
            rows = pl.ds(b * BLK, BLK)
            k0 = normalize(k_s[h, rows, 0:128])
            k1 = normalize(k_s[h, rows, 128:256])
            v0 = v_s[h, rows, 0:128]
            v1 = v_s[h, rows, 128:256]
            c0, c1 = b0[b * BLK:(b + 1) * BLK], b1[b * BLK:(b + 1) * BLK]
            keys = interleave(k0, k1)
            bkeys = interleave(c0 * k0, c1 * k1)
            bvals = interleave(c0 * v0, c1 * v1)
            kt = jnp.transpose(keys)
            a = mm3(bkeys, kt) * mask_s[b]
            tcol = tid_s[b]
            live = jnp.where(tcol == edge_s[b, 0], 1.0, 0.0)
            rhs.append(jnp.concatenate([-(interleave(live, live) * bkeys), bvals], axis=1))
            kt_s[h, b] = kt
            kts.append(kt)
            systems.append(a)
            for half in range(2):
                lo = half * 128
                acc = jnp.zeros((16, 128), F32)
                lanes = iota((16, 128), 1) // 16
                for g in range(8):
                    acc = acc + jnp.where(lanes == g, a[lo + g * 16:lo + (g + 1) * 16, lo:lo + 128], 0.0)
                cs_s[:, 2 * b + half, :] = acc
        flat = cs_s[...].reshape(128, 128)
        hi, low = halves(flat)
        bc_s[...] = dot(hi, spread_s[...]) + dot(low, spread_s[...])
        solved = {}
        order = [j * 8 + t for t in range(8) for j in range(2)]
        unit = iota((8, 128), 1) % 16
        for place, i in enumerate(order):
            x = jnp.where(unit == i, 1.0, 0.0)
            for j in order[:place]:
                x = x - bc_s[i * 8:(i + 1) * 8, j * 128:(j + 1) * 128] * solved[j]
            solved[i] = x
            xs_s[i] = x
        for b in range(NB):
            a = systems[b]
            ts = []
            for half in range(2):
                lo = half * 128
                x = xs_s[:, 2 * b + half, :]
                t = jnp.where(r128 // 16 == c128 // 16, jnp.concatenate([x] * 8, axis=0), 0.0)
                for size in (16, 32, 64):
                    t = level(t, a[lo:lo + 128, lo:lo + 128], size)
                ts.append(t)
            u1 = mm3(ts[0], rhs[b][:128])
            u2 = mm3(ts[1], rhs[b][128:] - mm3(a[128:, :128], u1))
            u = jnp.concatenate([u1, u2], axis=0)
            u_s[h, b] = u
            tcol = tid_s[b]
            ending = jnp.where(tcol == edge_s[b, 1], 1.0, 0.0)
            ending = interleave(ending, ending)
            lw = mm3(kts[b], jnp.concatenate([ending, ending], axis=1) * u)
            through = jnp.where(edge_s[b, 0] == edge_s[b, 1], eye, 0.0)
            lift = lw[:, :128] + through
            write = lw[:, 128:]
            if b == 0:
                pair = jnp.concatenate([lift, write], axis=1)
            else:
                pair = mm3(lift, pair)
                pair = jnp.concatenate([pair[:, :128], pair[:, 128:] + write], axis=1)
            if b < NB - 1:
                pre_s[h, b] = pair
        send_s[h] = pair.astype(BF16)
        return carry

    def exchange(h):
        copies = [
            remote(send_s.at[h], recv_s.at[step - 1, h], esend.at[step - 1, h], erecv.at[step - 1, h], at(step, core))
            for step in (1, 2, 3)
        ]
        copies.append(
            remote(send_s.at[h, :, pl.ds(128, 128)], wrecv_s.at[h], esend.at[3, h], erecv.at[3, h], at(4, core))
        )
        return copies

    def maps_and_send(h, carry):
        maps(h, carry)
        for c in exchange(h):
            c.start()
        return carry

    lax.fori_loop(0, HERE, maps_and_send, 0)

    def local_out(h, carry):
        for b in range(NB):
            rows = pl.ds(b * BLK, BLK)
            q = normalize(q_s[rows, pl.ds(pl.multiple_of(h * 128, 128), 128)])
            scores = mm3(q, kt_s[h, b]) * vis_s[b]
            res = mm3(scores, u_s[h, b])
            live = jnp.where(tid_s[b] == edge_s[b, 0], q, 0.0)
            thr, loc = res[:, :128] + live, res[:, 128:]
            if b > 0:
                res = mm3(thr, pre_s[h, b - 1])
                thr, loc = res[:, :128], res[:, 128:] + loc
            thr_s[h, rows, :] = jnp.concatenate([thr, loc], axis=1)
        return carry

    lax.fori_loop(0, HERE, local_out, 0)
    local[8].wait()

    for h in range(HERE):
        for c in exchange(h):
            c.wait()
        state = wrecv_s[h].astype(F32)
        for step in (3, 2, 1):
            state = mm3(recv_s[step - 1, h, :, 0:128].astype(F32), state) + recv_s[step - 1, h, :, 128:256].astype(F32)
        for part in range(2):
            rows = pl.ds(part * 256, 256)
            o = thr_s[h, rows, 128:256] + mm3(thr_s[h, rows, 0:128], state)
            o = o * lax.rsqrt(jnp.mean(o * o, axis=-1, keepdims=True) + norm_eps)
            g = gain[:, pl.ds(pl.multiple_of(core * 256 + h * 128, 128), 128)]
            hid_s[part, :, h * 128:(h + 1) * 128] = (o * g).astype(BF16)

    swap_hid = remote(hid_s.at[other], hid2_s.at[core], hsem.at[0], hsem.at[1], at(0, other))
    swap_hid.start()
    hid2_s[core] = hid_s[core]
    swap_hid.wait()

    def term(step):
        rows = pl.ds(pl.multiple_of(lax.rem(head + step + nhead, nhead) * 64, 64), 64)
        return lambda cols: (
            dot(hid2_s[0, rows, :], wo_s[0:256, cols]) + dot(hid2_s[1, rows, :], wo_s[256:512, cols])
        ).astype(BF16)

    A, B = slice(0, 1024), slice(1024, 2048)
    part = (A, B)
    def hop(direction, stage):
        return remote(
            rs_s.at[direction, stage], rr_s.at[direction, stage], rsend.at[direction, stage], rrecv.at[direction, stage],
            along(1 if direction == 0 else -1),
        )

    far = term(2)
    for d in range(2):
        rs_s[d, 0] = far(part[d])
        hop(d, 0).start()
    near = (term(1), term(-1))
    for d in range(2):
        rs_s[d, 1] = near[d](part[1 - d])
        hop(d, 1).start()
    for d in range(2):
        mine = near[d](part[d]).astype(F32)
        hop(d, 0).wait()
        rs_s[d, 2] = (mine + rr_s[d, 0].astype(F32)).astype(BF16)
        hop(d, 2).start()
    own = term(0)
    sums = [own(p).astype(F32) for p in part]
    for d in range(2):
        hop(d, 1).wait()
        sums[1 - d] = sums[1 - d] + rr_s[d, 1].astype(F32)
    for d in range(2):
        hop(d, 2).wait()
        sums[d] = sums[d] + rr_s[d, 2].astype(F32)
    out[:, A] = sums[0].astype(BF16)
    out[:, B] = sums[1].astype(BF16)


def body(tokens, turn_ids, q_weight, k_weight, v_weight, beta_weight, beta_bias, norm_gain, out_weight):
    any_ = pl.BlockSpec(memory_space=pl.ANY)
    vmem = pl.BlockSpec(memory_space=pltpu.VMEM)
    V = pltpu.VMEM
    D = tokens.shape[1]
    return pl.pallas_call(
        kernel,
        out_shape=jax.ShapeDtypeStruct((64, 2048), BF16),
        in_specs=[any_] * 6 + [vmem, vmem, any_],
        out_specs=vmem,
        scratch_shapes=[
            V((512, D), BF16), V((2, D, 256), BF16), V((2, D, 256), BF16), V((D, 256), BF16), V((D, 8), BF16),
            V((512, D), BF16), V((2, 2, 128), jnp.int32), V((2, 2, 128), jnp.int32),
            V((2, 512, 256), F32), V((2, 512, 256), F32), V((512, 256), F32), V((512, 8), F32),
            V((NB, 256, 256), F32), V((NB, 128, 256), F32), V((NB, 128, 128), F32), V((NB, 2, 128, 128), F32),
            V((128, 2048), BF16),
            V((16, 8, 128), F32), V((128, 2048), F32), V((16, 8, 128), F32),
            V((2, NB, 256, 256), F32), V((2, NB, 128, 256), F32), V((2, NB - 1, 128, 256), F32), V((2, 512, 256), F32),
            V((2, 128, 256), BF16), V((3, 2, 128, 256), BF16), V((2, 128, 128), BF16),
            V((2, 256, 256), BF16), V((2, 256, 256), BF16),
            V((2, 3, 64, 1024), BF16), V((2, 3, 64, 1024), BF16),
            pltpu.SemaphoreType.DMA((9,)), pltpu.SemaphoreType.DMA((2,)), pltpu.SemaphoreType.DMA((6,)),
            pltpu.SemaphoreType.DMA((4, 2)), pltpu.SemaphoreType.DMA((4, 2)), pltpu.SemaphoreType.DMA((2,)),
            pltpu.SemaphoreType.DMA((2, 3)), pltpu.SemaphoreType.DMA((2, 3)),
        ],
        compiler_params=pltpu.CompilerParams(
            collective_id=0, has_side_effects=True, vmem_limit_bytes=56 * 1024 * 1024
        ),
        cost_estimate=pl.CostEstimate(flops=5_000_000_000, bytes_accessed=14_000_000, transcendentals=10_000),
    )(
        tokens, turn_ids.reshape(2, 128), q_weight, k_weight, v_weight, beta_weight,
        beta_bias.reshape(1, 8), norm_gain.reshape(1, 512), out_weight,
    )


def solution(mesh):
    return jax.shard_map(
        body,
        mesh=mesh,
        in_specs=(
            P("seq", None),
            P("seq"),
            P(None, "head"),
            P(None, "head"),
            P(None, "head"),
            P(None, "head"),
            P("head"),
            P("head"),
            P("head", None),
        ),
        out_specs=P(("seq", "head"), None),
        check_vma=False,
    )
```

time: 423 us -> 59.9 us (0.14)
  other arithmetic: 176 us -> 0 us
  waiting for transfers between devices: 102 us -> 0 us
  matrix products: 98.4 us -> 0 us
  Pallas kernels: 0 us -> 56.2 us
  local copies, waits for them, and re-layouts: 24.6 us -> 3.43 us
  between operations: 13.5 us -> 0.01 us
  starting transfers between devices: 4.67 us -> 0 us
    another operation x1 -> x0, other arithmetic: 159 us -> none  [span_terms(): jax.scipy.linalg.solve_triangular(system, jnp.diag(betas), lower=True)]
    dot_general x55 -> x0, matrix products: 95.1 us -> none  [the longest x40 54.2 us: matmul_heads(): jnp.einsum('hij,hjk->hik', left, right, precision=lax.Precision.HIGHEST)]
    all_gather x2 -> x0, waiting for transfers between devices: 80.2 us -> none  [prefix(): lax.all_gather(part.astype(kind), axis)]
    pallas_call x0 -> x1, Pallas kernels: none -> 56.2 us  [body(): pl.pallas_call(kernel, out_shape=jax.ShapeDtypeStruct((64, 2048), BF16),...]
    reduce_scatter x1 -> x0, waiting for transfers between devices: 21.3 us -> none  [body(): lax.psum_scatter(jnp.dot(hidden, out_weight, preferred_element_type=jnp.f...]
    reshape x5 -> x0, local copies, waits for them, and re-layouts: 7.41 us -> none  [the longest x1 3.07 us: project(): jnp.dot(tokens, v_weight, preferred_element_type=jnp.float32)]
    ppermute x1 -> x0, starting transfers between devices: 4.58 us -> none  [shifted(): return lax.ppermute(block, axis, route)]
    while x40 -> x0, local copies, waits for them, and re-layouts: 4.49 us -> none
  transfers between devices with their start and end apart: 4 -> 0, of which waited for: 3 -> 0; matrix products, arithmetic and copies ran while one was open for 51% -> 0% of each run, Pallas kernels for 0% -> 0%
where the time goes in v1:
time: 59.9 us; the launch traced here: 59.7 us
  Pallas kernels  56.2 us (94%)
  local copies, waits for them, and re-layouts  3.43 us (6%)
    pallas_call x1, Pallas kernels, body(): pl.pallas_call(kernel, out_shape=jax.ShapeDtypeStruct((64, 2048), BF16),...  56.2 us
    unnamed x2, local copies, waits for them, and re-layouts  3.43 us

profile of v1, /device:TPU:1, one launch (start us, length us, event | category | flops | bytes accessed | tf_op | source)
XLA Modules:
  0.0 59.7 jit_solution(12849118479951883330)
XLA Ops:
  0.0 1.8 %copy.10.bw = bf16[2048,8]{1,0:T(8,128)(2,1)} copy(bf16[2048,8]{0,1:T(8,128)(2,1)} %param.14) | data formatting | bytes 65536 | tf_op args[5]
  1.8 56.2 %shard_map.91 = bf16[64,2048]{1,0:T(8,128)(2,1)} custom-call(bf16[256,2048]{1,0:T(8,128)(2,1)} %tok.1, s32[2,128]{1,0:T(2,128)} %bitcast.4, bf16[2048,512]{1,0:T(8,128)(2,1)} %qw.1, bf16[2048,1024]{1,0:T(8,128)(2,1)} %kw.1, bf16[2048,1024]{1,0:T(8,128)(2,1)} %vw.1, bf16[2048,8]{1,0:T(8,128)(2,1)} %copy.10.bw, f32[1,8]{1,0:T(1,128)} %bitcast.5, ...), custom_call_target="tpu_custom_call" | custom-call | flops 5000000000 | bytes 14000000 | tf_op jit(solution)/shard_map/pallas_call | solution.py:362
  58.0 1.7 %copy.12 = bf16[64,2048]{1,0:T(8,128)(2,1)} copy(bf16[64,2048]{1,0:T(8,128)(2,1)} %shard_map.91) | data formatting | bytes 524288

commit v2 on v0

v2 whole, which is shorter than its diff:
```python
import functools

import jax
import jax.numpy as jnp
from jax import lax
from jax.experimental import pallas as pl
from jax.experimental.pallas import tpu as pltpu
from jax.sharding import PartitionSpec as P

F32, BF16 = jnp.float32, jnp.bfloat16
MESH = pl.DeviceIdType.MESH
DK = 128
BLK = 128
REFL = 2 * BLK
NB = 4
HERE = 2
REACH = 4
key_eps = 1e-06
norm_eps = 1e-05

NN = (((1,), (0,)), ((), ()))
NT = (((1,), (1,)), ((), ()))


def dot(a, b, dims=NN):
    return lax.dot_general(a, b, dims, preferred_element_type=F32)


def halves(a):
    hi = a.astype(BF16)
    return hi, (a - hi.astype(F32)).astype(BF16)


def joined(a, b):
    (ah, al), (bh, bl) = a, b
    return dot(jnp.concatenate([ah, al, ah], axis=1), jnp.concatenate([bh, bh, bl], axis=0))


def mm3(a, b):
    return joined(halves(a), halves(b))


def iota(shape, axis):
    return lax.broadcasted_iota(jnp.int32, shape, axis)


def interleave(a, b):
    groups, lanes = a.shape[0] // 8, a.shape[1]
    return jnp.concatenate(
        [a.reshape(groups, 1, 8, lanes), b.reshape(groups, 1, 8, lanes)], axis=1
    ).reshape(groups * 16, lanes)


def token_of(r):
    return (r // 16) * 8 + r % 8


def time_of(r):
    return token_of(r) * 2 + (r // 8) % 2


def normalize(v):
    return v * lax.rsqrt(jnp.sum(v * v, axis=-1, keepdims=True) + key_eps)


def kernel(
    tok, ids, qw, kw, vw, bw, bb, gain, ow,
    out,
    x_s, wk_s, wv_s, wq_s, bw_s, wo_s, ids_s, prev_s,
    k_s, v_s, q_s, beta_s, tid_s, vis_s, mask_s, end_s, spread_s,
    cs_s, bc_s, xs_s, u_s, kt_s, lw_s, duo_s, thr_s,
    send_s, recv_s, wrecv_s, hid_s, hid2_s, far_s, wf_s, rs_s, rr_s,
    lsem, tsem, isem, esend, erecv, hsem, fsem, wsem, rsend, rrecv,
):
    seq = lax.axis_index("seq")
    head = lax.axis_index("head")
    nseq = lax.axis_size("seq")
    nhead = lax.axis_size("head")
    chips = nseq // 2
    chip, core = seq // 2, lax.rem(seq, 2)
    other = 1 - core

    def at(step, which):
        return (lax.rem(chip + step + chips, chips) * 2 + which, head)

    def along(step):
        return (seq, lax.rem(head + step + nhead, nhead))

    def across(step):
        return (chip * 2 + other, lax.rem(head + step + nhead, nhead))

    own_rows = pl.ds(pl.multiple_of(core * 256, 256), 256)
    def weights(ref, width, h):
        return ref.at[:, pl.ds(pl.multiple_of(core * HERE * width + h * width, 256), 256)]

    X, K0, BW, V0, K1, V1, Q, O, IDS = range(9)
    pairs = [
        (tok, x_s.at[own_rows]), (weights(kw, 256, 0), wk_s.at[0]), (bw, bw_s), (weights(vw, 256, 0), wv_s.at[0]),
        (weights(kw, 256, 1), wk_s.at[1]), (weights(vw, 256, 1), wv_s.at[1]), (weights(qw, 128, 0), wq_s), (ow, wo_s),
        (ids, ids_s.at[core]),
    ]
    local = [pltpu.make_async_copy(src, dst, lsem.at[n]) for n, (src, dst) in enumerate(pairs)]
    for c in local:
        c.start()

    barrier = pltpu.get_barrier_semaphore()
    mutual = [at(0, other), along(1), along(-1), along(2), across(2)]
    for peer in mutual:
        pl.semaphore_signal(barrier, inc=1, device_id=peer, device_id_type=MESH)
    for step in range(1, REACH + 1):
        @pl.when(chip >= step)
        def _():
            pl.semaphore_signal(barrier, inc=1, device_id=at(-step, core), device_id_type=MESH)
            if step == 1:
                pl.semaphore_signal(barrier, inc=1, device_id=at(-step, other), device_id_type=MESH)
    greeted = len(mutual) + jnp.minimum(chips - 1 - chip, REACH) + jnp.minimum(chips - 1 - chip, 1)

    def remote(src, dst, ssem, rsem, peer):
        return pltpu.make_async_remote_copy(
            src_ref=src, dst_ref=dst, send_sem=ssem, recv_sem=rsem, device_id=peer, device_id_type=MESH
        )

    swap_ids = remote(ids, ids_s.at[core], isem.at[0], isem.at[1], at(0, other))
    swap_tok = remote(tok, x_s.at[own_rows], tsem.at[0], tsem.at[1], at(0, other))
    next_same = remote(ids, prev_s.at[core], isem.at[2], isem.at[3], at(1, core))
    half_rows = pl.ds(pl.multiple_of(core * 256, 256), 256)
    far_weights = remote(ow.at[half_rows], wf_s.at[half_rows], wsem.at[0], wsem.at[1], along(2))
    pass_weights = remote(wf_s.at[half_rows], wf_s.at[half_rows], wsem.at[2], wsem.at[3], at(0, other))
    next_other = remote(ids, prev_s.at[core], isem.at[4], isem.at[5], at(1, other))

    sr, sc = iota((128, 2048), 0), iota((128, 2048), 1)
    spread_s[...] = ((sr // 16 == (sc % 128) // 16) & (sr % 16 == sc // 128)).astype(F32).astype(BF16)

    def rows_of(half):
        return pl.ds(pl.multiple_of(half * 256, 256), 256)

    def project(rows, h):
        x = x_s[rows, :]
        k_s[h, rows, :] = dot(x, wk_s[h])
        v_s[h, rows, :] = dot(x, wv_s[h])

    def strengths(rows):
        beta_s[rows, :] = 2.0 * jax.nn.sigmoid(dot(x_s[rows, :], bw_s[...], NT) + bb[...])

    r128, c128 = iota((128, 128), 0), iota((128, 128), 1)
    eye = (r128 == c128).astype(F32)
    rr_, cc_ = iota((REFL, REFL), 0), iota((REFL, REFL), 1)
    earlier = time_of(rr_) > time_of(cc_)
    seen = token_of(iota((BLK, REFL), 1)) <= iota((BLK, REFL), 0)
    lanes16 = iota((16, 128), 1) // 16
    unit8 = iota((8, 128), 1) % 16
    order = [j * 8 + t for t in range(8) for j in range(2)]

    def odd_rows(m, size):
        return jnp.concatenate([m[i * size:(i + 1) * size] for i in range(1, 128 // size, 2)], axis=0)

    def even_rows(m, size):
        return jnp.concatenate([m[i * size:(i + 1) * size] for i in range(0, 128 // size, 2)], axis=0)

    def merged(even, odd, size):
        return jnp.concatenate(
            [m[i * size:(i + 1) * size] for i in range(64 // size) for m in (even, odd)], axis=0
        )

    def turns(half):
        for j in range(2):
            row = ids_s[half, pl.ds(j, 1), :].astype(F32)
            tcol = jnp.transpose(jnp.broadcast_to(row, (BLK, BLK)))
            rcol = interleave(tcol, tcol)
            rrow = jnp.transpose(rcol)
            mask_s[half, j] = jnp.where(
                earlier & (jnp.concatenate([rcol, rcol], axis=1) == jnp.concatenate([rrow, rrow], axis=0)), 1.0, 0.0
            )
            end_s[half, j] = jnp.where(rrow[:16] == jnp.max(row, axis=1, keepdims=True), 1.0, 0.0)
            vis_s[half, j] = jnp.where(seen & (jnp.concatenate([tcol, tcol], axis=1) == rrow), 1.0, 0.0)
            tid_s[half, j] = tcol

    def maps(units):
        systems, rhs, kts = [], [], []
        for half, h, j in units:
            block = pl.ds(pl.multiple_of(half * 256 + j * BLK, BLK), BLK)
            betas = beta_s[block, :]
            lane = iota(betas.shape, 1)
            mine = [
                jnp.sum(jnp.where(lane == core * 4 + h * 2 + r, betas, 0.0), axis=1, keepdims=True) for r in range(2)
            ]
            k0 = normalize(k_s[h, block, 0:128])
            k1 = normalize(k_s[h, block, 128:256])
            keys = interleave(k0, k1)
            bkeys = interleave(mine[0] * k0, mine[1] * k1)
            bvals = interleave(mine[0] * v_s[h, block, 0:128], mine[1] * v_s[h, block, 128:256])
            kt = halves(jnp.transpose(keys))
            kt_s[half, h, j, 0] = kt[0]
            kt_s[half, h, j, 1] = kt[1]
            systems.append(joined(halves(bkeys), kt) * mask_s[half, j])
            rhs.append(jnp.concatenate([-bkeys, bvals], axis=1))
            ending = end_s[half, j][:1].astype(BF16)
            kts.append((kt[0] * ending, kt[1] * ending))
        tiles = [a[lo:lo + 128, lo:lo + 128] for a in systems for lo in (0, 128)]
        for n, a in enumerate(tiles):
            acc = jnp.where(lanes16 == 0, a[0:16], 0.0)
            for g in range(1, 8):
                acc = jnp.where(lanes16 == g, a[g * 16:(g + 1) * 16], acc)
            for slot in range(n, 8, len(tiles)):
                cs_s[:, slot, :] = acc
        hi, low = halves(cs_s[...].reshape(128, 128))
        bc_s[...] = dot(hi, spread_s[...]) + dot(low, spread_s[...])
        solved = {}
        for place, i in enumerate(order):
            x = jnp.where(unit8 == i, 1.0, 0.0)
            for j in order[:place]:
                x = x - bc_s[i * 8:(i + 1) * 8, j * 128:(j + 1) * 128] * solved[j]
            solved[i] = x
            xs_s[i] = x
        ts = [
            jnp.where(r128 // 16 == c128 // 16, jnp.concatenate([xs_s[:, n, :]] * 8, axis=0), 0.0)
            for n in range(len(tiles))
        ]
        for size in (16, 32, 64):
            ro = odd_rows(r128, size)
            pick = (ro // (2 * size) == c128[:64] // (2 * size)) & ((c128[:64] // size) % 2 == 0)
            split = [halves(t) for t in ts]
            lows = [
                joined(halves(jnp.where(pick, odd_rows(a, size), 0.0)), t) for a, t in zip(tiles, split)
            ]
            zero = jnp.zeros((64, 128), F32)
            news = [
                joined((odd_rows(t[0], size), odd_rows(t[1], size)), halves(merged(zero, low, size)))
                for t, low in zip(split, lows)
            ]
            ts = [merged(even_rows(t, size), odd_rows(t, size) - new, size) for t, new in zip(ts, news)]
        split = [halves(t) for t in ts]
        tops = [joined(split[2 * n], halves(rhs[n][:128])) for n in range(len(units))]
        mids = [
            rhs[n][128:] - joined(halves(systems[n][128:, :128]), halves(tops[n])) for n in range(len(units))
        ]
        lows = [joined(split[2 * n + 1], halves(mids[n])) for n in range(len(units))]
        lws = []
        for n, (half, h, j) in enumerate(units):
            u = halves(jnp.concatenate([tops[n], lows[n]], axis=0))
            u_s[half, h, j, 0] = u[0]
            u_s[half, h, j, 1] = u[1]
            lws.append(joined(kts[n], u))
        for n, (half, h, j) in enumerate(units):
            last = jnp.max(ids_s[half, pl.ds(j, 1), :].astype(F32), axis=1, keepdims=True)
            lift = jnp.where(before(half, j) == last, eye + lws[n][:, :128], 0.0)
            lws[n] = jnp.concatenate([lift, lws[n][:, 128:]], axis=1)
            lw_s[half, h, j] = lws[n]
        for n, (half, h, j) in enumerate(units):
            if j == 1:
                duo_s[half, h] = after(lws[n], lws[n - 1])

    def after(late, early):
        pair = mm3(late[:, :128], early)
        return jnp.concatenate([pair[:, :128], pair[:, 128:] + late[:, 128:]], axis=1)

    def before(half, j):
        if j == 1:
            return jnp.max(ids_s[half, pl.ds(0, 1), :].astype(F32), axis=1, keepdims=True)
        first = jnp.max(prev_s[1, pl.ds(1, 1), :].astype(F32), axis=1, keepdims=True)
        first = jnp.where(chip == 0, -1.0, first)
        inner = jnp.max(ids_s[0, pl.ds(1, 1), :].astype(F32), axis=1, keepdims=True)
        return jnp.where(half == 0, first, inner)

    def exchange(h, step):
        if step == REACH:
            return remote(
                send_s.at[h, :, pl.ds(128, 128)], wrecv_s.at[h], esend.at[step - 1, h], erecv.at[step - 1, h], at(step, core)
            )
        return remote(
            send_s.at[h], recv_s.at[step - 1, h], esend.at[step - 1, h], erecv.at[step - 1, h], at(step, core)
        )

    def send_maps(h):
        send_s[h] = after(duo_s[1, h], duo_s[0, h]).astype(BF16)
        for step in range(1, REACH + 1):
            @pl.when(chip + step < chips)
            def _():
                exchange(h, step).start()

    for n in (X, K0, V0):
        local[n].wait()
    project(rows_of(core), 0)
    pl.semaphore_wait(barrier, greeted)
    for c in (swap_ids, swap_tok, far_weights):
        c.start()

    @pl.when(chip + 1 < chips)
    def _():
        next_same.start()
        next_other.start()

    for step in range(1, REACH + 1):
        @pl.when(chip < step)
        def _():
            if step == REACH:
                wrecv_s[...] = jnp.zeros_like(wrecv_s)
            else:
                recv_s[step - 1] = jnp.zeros(recv_s.shape[1:], BF16)
            if step == 1:
                prev_s[...] = jnp.zeros_like(prev_s)

    for n in (BW, IDS):
        local[n].wait()
    strengths(rows_of(core))
    turns(core)
    swap_ids.wait()

    @pl.when(chip >= 1)
    def _():
        next_same.wait_recv()
        next_other.wait_recv()

    maps([(core, 0, 0), (core, 0, 1)])
    turns(other)
    swap_tok.wait()
    project(rows_of(other), 0)
    strengths(rows_of(other))
    maps([(other, 0, 0), (other, 0, 1)])
    send_maps(0)
    for n in (K1, V1):
        local[n].wait()
    project(slice(None), 1)
    maps([(0, 1, 0), (0, 1, 1), (1, 1, 0), (1, 1, 1)])
    send_maps(1)

    local[Q].wait()
    q_s[...] = dot(x_s[...], wq_s[...])

    def local_out(h, carry):
        second = duo_s[0, h]
        pre = (None, lw_s[0, h, 0], second, after(lw_s[1, h, 0], second))
        blocks = [(b // 2, b % 2) for b in range(NB)]
        qs = [
            normalize(q_s[pl.ds(b * BLK, BLK), pl.ds(pl.multiple_of(h * 128, 128), 128)]) for b in range(NB)
        ]
        scores = [
            joined(halves(qs[b]), (kt_s[p, h, j, 0], kt_s[p, h, j, 1])) * vis_s[p, j] for b, (p, j) in enumerate(blocks)
        ]
        res = [
            joined(halves(scores[b]), (u_s[p, h, j, 0], u_s[p, h, j, 1])) for b, (p, j) in enumerate(blocks)
        ]
        for b, (p, j) in enumerate(blocks):
            thr = jnp.where(tid_s[p, j] == before(p, j), qs[b] + res[b][:, :128], 0.0)
            loc = res[b][:, 128:]
            if b > 0:
                both = mm3(thr, pre[b])
                thr, loc = both[:, :128], both[:, 128:] + loc
            thr_s[h, pl.ds(b * BLK, BLK), :] = jnp.concatenate([thr, loc], axis=1)
        return carry

    lax.fori_loop(0, HERE, local_out, 0)
    local[O].wait()
    far_weights.wait()
    pass_weights.start()

    states = []
    for h in range(HERE):
        for step in range(1, REACH + 1):
            @pl.when(chip >= step)
            def _():
                exchange(h, step).wait_recv()
        state = wrecv_s[h].astype(F32)
        for step in (3, 2, 1):
            state = mm3(recv_s[step - 1, h, :, 0:128].astype(F32), state) + recv_s[step - 1, h, :, 128:256].astype(F32)
        states.append(halves(state))

    def outputs(half):
        done = []
        for h in range(HERE):
            both = thr_s[h, rows_of(half), :]
            o = both[:, 128:] + joined(halves(both[:, :128]), states[h])
            o = o * lax.rsqrt(jnp.mean(o * o, axis=-1, keepdims=True) + norm_eps)
            g = gain[:, pl.ds(pl.multiple_of(core * 256 + h * 128, 128), 128)]
            done.append((o * g).astype(BF16))
        return jnp.concatenate(done, axis=1)

    far_rows = pl.ds(pl.multiple_of(lax.rem(head + 2, nhead) * 64, 64), 64)
    hid_s[...] = outputs(other)
    swap_hid = remote(hid_s, hid2_s.at[core], hsem.at[0], hsem.at[1], at(0, other))
    swap_hid.start()
    far_other = remote(hid_s.at[far_rows], far_s.at[core], fsem.at[0], fsem.at[1], across(2))
    far_other.start()
    hid2_s[core] = outputs(core)
    far_same = remote(hid2_s.at[core, far_rows], far_s.at[core], fsem.at[2], fsem.at[3], along(2))
    far_same.start()
    swap_hid.wait()

    def term(step, cols):
        rows = pl.ds(pl.multiple_of(lax.rem(head + step + nhead, nhead) * 64, 64), 64)
        return dot(hid2_s[0, rows, :], wo_s[0:256, cols]) + dot(hid2_s[1, rows, :], wo_s[256:512, cols])

    parts = [slice(n * 512, (n + 1) * 512) for n in range(4)]

    def hop(d, n):
        return remote(rs_s.at[d, n], rr_s.at[d, n], rsend.at[d, n], rrecv.at[d, n], along(1 if d == 0 else -1))

    for n, cols in enumerate(parts):
        for d in range(2):
            rs_s[d, n] = term(1 if d == 0 else -1, cols).astype(BF16)
            hop(d, n).start()
    sums = [term(0, cols).astype(BF16).astype(F32) for cols in parts]
    pass_weights.wait()
    far_other.wait()
    far_same.wait()
    far = [far_s[0], far_s[1]]
    for n, cols in enumerate(parts):
        extra = dot(far[0], wf_s[0:256, cols]) + dot(far[1], wf_s[256:512, cols])
        sums[n] = sums[n] + extra.astype(BF16).astype(F32)
    for n, cols in enumerate(parts):
        for d in range(2):
            hop(d, n).wait()
            sums[n] = sums[n] + rr_s[d, n].astype(F32)
        out[:, cols] = sums[n].astype(BF16)
    for step in range(1, REACH + 1):
        @pl.when(chip + step < chips)
        def _():
            for h in range(HERE):
                exchange(h, step).wait_send()

    @pl.when(chip + 1 < chips)
    def _():
        next_same.wait_send()
        next_other.wait_send()


def body(tokens, turn_ids, q_weight, k_weight, v_weight, beta_weight, beta_bias, norm_gain, out_weight):
    any_ = pl.BlockSpec(memory_space=pl.ANY)
    vmem = pl.BlockSpec(memory_space=pltpu.VMEM)
    V = pltpu.VMEM
    D = tokens.shape[1]
    return pl.pallas_call(
        kernel,
        out_shape=jax.ShapeDtypeStruct((64, 2048), BF16),
        in_specs=[any_] * 6 + [vmem, vmem, any_],
        out_specs=vmem,
        scratch_shapes=[
            V((512, D), BF16), V((2, D, 256), BF16), V((2, D, 256), BF16), V((D, 256), BF16), V((8, D), BF16),
            V((512, D), BF16), V((2, 2, 128), jnp.int32), V((2, 2, 128), jnp.int32),
            V((2, 512, 256), F32), V((2, 512, 256), F32), V((512, 256), F32), V((512, 8), F32),
            V((2, 2, 128, 128), F32), V((2, 2, 128, 256), F32), V((2, 2, 256, 256), F32), V((2, 2, 16, 256), F32), V((128, 2048), BF16),
            V((16, 8, 128), F32), V((128, 2048), F32), V((16, 8, 128), F32),
            V((2, 2, 2, 2, 256, 256), BF16), V((2, 2, 2, 2, 128, 256), BF16), V((2, 2, 2, 128, 256), F32),
            V((2, 2, 128, 256), F32), V((2, 512, 256), F32),
            V((2, 128, 256), BF16), V((3, 2, 128, 256), BF16), V((2, 128, 128), BF16),
            V((256, 256), BF16), V((2, 256, 256), BF16),
            V((2, 64, 256), BF16), V((512, D), BF16), V((2, 4, 64, 512), BF16), V((2, 4, 64, 512), BF16),
            *[
                pltpu.SemaphoreType.DMA(shape)
                for shape in ((9,), (2,), (6,), (4, 2), (4, 2), (2,), (4,), (4,), (2, 4), (2, 4))
            ],
        ],
        compiler_params=pltpu.CompilerParams(
            collective_id=0, has_side_effects=True, vmem_limit_bytes=56 * 1024 * 1024
        ),
        cost_estimate=pl.CostEstimate(flops=5_000_000_000, bytes_accessed=14_000_000, transcendentals=10_000),
    )(
        tokens, turn_ids.reshape(2, 128), q_weight, k_weight, v_weight, beta_weight.T,
        beta_bias.reshape(1, 8), norm_gain.reshape(1, 512), out_weight,
    )


def solution(mesh):
    return jax.shard_map(
        body,
        mesh=mesh,
        in_specs=(
            P("seq", None),
            P("seq"),
            P(None, "head"),
            P(None, "head"),
            P(None, "head"),
            P(None, "head"),
            P("head"),
            P("head"),
            P("head", None),
        ),
        out_specs=P(("seq", "head"), None),
        check_vma=False,
    )
```

time: 423 us -> 44.6 us (0.11)
  other arithmetic: 176 us -> 0 us
  waiting for transfers between devices: 102 us -> 0 us
  matrix products: 98.4 us -> 0 us
  Pallas kernels: 0 us -> 42.7 us
  local copies, waits for them, and re-layouts: 24.6 us -> 1.67 us
  between operations: 13.5 us -> 0.01 us
  starting transfers between devices: 4.67 us -> 0 us
    another operation x1 -> x0, other arithmetic: 159 us -> none  [span_terms(): jax.scipy.linalg.solve_triangular(system, jnp.diag(betas), lower=True)]
    dot_general x55 -> x0, matrix products: 95.1 us -> none  [the longest x40 54.2 us: matmul_heads(): jnp.einsum('hij,hjk->hik', left, right, precision=lax.Precision.HIGHEST)]
    all_gather x2 -> x0, waiting for transfers between devices: 80.2 us -> none  [prefix(): lax.all_gather(part.astype(kind), axis)]
    pallas_call x0 -> x1, Pallas kernels: none -> 42.7 us  [body(): pl.pallas_call(kernel, out_shape=jax.ShapeDtypeStruct((64, 2048), BF16),...]
    reduce_scatter x1 -> x0, waiting for transfers between devices: 21.3 us -> none  [body(): lax.psum_scatter(jnp.dot(hidden, out_weight, preferred_element_type=jnp.f...]
    reshape x5 -> x0, local copies, waits for them, and re-layouts: 7.41 us -> none  [the longest x1 3.07 us: project(): jnp.dot(tokens, v_weight, preferred_element_type=jnp.float32)]
    ppermute x1 -> x0, starting transfers between devices: 4.58 us -> none  [shifted(): return lax.ppermute(block, axis, route)]
    while x40 -> x0, local copies, waits for them, and re-layouts: 4.49 us -> none
  transfers between devices with their start and end apart: 4 -> 0, of which waited for: 3 -> 0; matrix products, arithmetic and copies ran while one was open for 51% -> 0% of each run, Pallas kernels for 0% -> 0%
where the time goes in v2:
time: 44.6 us; the launch traced here: 44.4 us
  Pallas kernels  42.7 us (96%)
  local copies, waits for them, and re-layouts  1.67 us (4%)
    pallas_call x1, Pallas kernels, body(): pl.pallas_call(kernel, out_shape=jax.ShapeDtypeStruct((64, 2048), BF16),...  42.7 us
    unnamed x1, local copies, waits for them, and re-layouts  1.67 us

profile of v2, /device:TPU:1, one launch (start us, length us, event | category | flops | bytes accessed | tf_op | source)
XLA Modules:
  0.0 44.4 jit_solution(11327878951362989774)
XLA Ops:
  0.0 42.7 %shard_map.91 = bf16[64,2048]{1,0:T(8,128)(2,1)} custom-call(bf16[256,2048]{1,0:T(8,128)(2,1)} %tok.1, s32[2,128]{1,0:T(2,128)} %bitcast.6, bf16[2048,512]{1,0:T(8,128)(2,1)} %qw.1, bf16[2048,1024]{1,0:T(8,128)(2,1)} %kw.1, bf16[2048,1024]{1,0:T(8,128)(2,1)} %vw.1, bf16[8,2048]{1,0:T(8,128)(2,1)} %bitcast.4, f32[1,8]{1,0:T(1,128)} %bitcast.7, ...), custom_call_target="tpu_custom_call" | custom-call | flops 5000000000 | bytes 14000000 | tf_op jit(solution)/shard_map/pallas_call | solution.py:432
  42.7 1.7 %copy.11 = bf16[64,2048]{1,0:T(8,128)(2,1)} copy(bf16[64,2048]{1,0:T(8,128)(2,1)} %shard_map.91) | data formatting | bytes 524288

commit v3 on v2

--- a/solution.py
+++ b/solution.py
@@ -14,6 +14,8 @@
 REFL = 2 * BLK
 NB = 4
 HERE = 2
+PARTS = [pl.ds(n * 512, 512) for n in range(4)]
+FETCHED = PARTS
 REACH = 4
 key_eps = 1e-06
 norm_eps = 1e-05
@@ -52,11 +54,11 @@
 
 
 def token_of(r):
-    return (r // 16) * 8 + r % 8
+    return ((r >> 4) << 3) + (r & 7)
 
 
 def time_of(r):
-    return token_of(r) * 2 + (r // 8) % 2
+    return token_of(r) * 2 + ((r >> 3) & 1)
 
 
 def normalize(v):
@@ -68,7 +70,7 @@
     out,
     x_s, wk_s, wv_s, wq_s, bw_s, wo_s, ids_s, prev_s,
     k_s, v_s, q_s, beta_s, tid_s, vis_s, mask_s, end_s, spread_s,
-    cs_s, bc_s, xs_s, u_s, kt_s, lw_s, duo_s, thr_s,
+    cs_s, bc_s, xs_s, u_s, kt_s, lw_s, duo_s, thr_s, loc_s,
     send_s, recv_s, wrecv_s, hid_s, hid2_s, far_s, wf_s, rs_s, rr_s,
     lsem, tsem, isem, esend, erecv, hsem, fsem, wsem, rsend, rrecv,
 ):
@@ -124,12 +126,18 @@
     swap_tok = remote(tok, x_s.at[own_rows], tsem.at[0], tsem.at[1], at(0, other))
     next_same = remote(ids, prev_s.at[core], isem.at[2], isem.at[3], at(1, core))
     half_rows = pl.ds(pl.multiple_of(core * 256, 256), 256)
-    far_weights = remote(ow.at[half_rows], wf_s.at[half_rows], wsem.at[0], wsem.at[1], along(2))
-    pass_weights = remote(wf_s.at[half_rows], wf_s.at[half_rows], wsem.at[2], wsem.at[3], at(0, other))
+    far_weights = [
+        remote(ow.at[half_rows, cols], wf_s.at[half_rows, cols], wsem.at[0, n], wsem.at[1, n], along(2))
+        for n, cols in enumerate(FETCHED)
+    ]
+    pass_weights = [
+        remote(wf_s.at[half_rows, cols], wf_s.at[half_rows, cols], wsem.at[2, n], wsem.at[3, n], at(0, other))
+        for n, cols in enumerate(FETCHED)
+    ]
     next_other = remote(ids, prev_s.at[core], isem.at[4], isem.at[5], at(1, other))
 
     sr, sc = iota((128, 2048), 0), iota((128, 2048), 1)
-    spread_s[...] = ((sr // 16 == (sc % 128) // 16) & (sr % 16 == sc // 128)).astype(F32).astype(BF16)
+    spread_s[...] = (((sr >> 4) == ((sc & 127) >> 4)) & ((sr & 15) == (sc >> 7))).astype(F32).astype(BF16)
 
     def rows_of(half):
         return pl.ds(pl.multiple_of(half * 256, 256), 256)
@@ -175,7 +183,7 @@
             vis_s[half, j] = jnp.where(seen & (jnp.concatenate([tcol, tcol], axis=1) == rrow), 1.0, 0.0)
             tid_s[half, j] = tcol
 
-    def maps(units):
+    def maps(units, arrived=lambda: None):
         systems, rhs, kts = [], [], []
         for half, h, j in units:
             block = pl.ds(pl.multiple_of(half * 256 + j * BLK, BLK), BLK)
@@ -241,6 +249,7 @@
             u_s[half, h, j, 0] = u[0]
             u_s[half, h, j, 1] = u[1]
             lws.append(joined(kts[n], u))
+        arrived()
         for n, (half, h, j) in enumerate(units):
             last = jnp.max(ids_s[half, pl.ds(j, 1), :].astype(F32), axis=1, keepdims=True)
             lift = jnp.where(before(half, j) == last, eye + lws[n][:, :128], 0.0)
@@ -281,8 +290,11 @@
     for n in (X, K0, V0):
         local[n].wait()
     project(rows_of(core), 0)
+    for n in (K1, V1):
+        local[n].wait()
+    project(rows_of(core), 1)
     pl.semaphore_wait(barrier, greeted)
-    for c in (swap_ids, swap_tok, far_weights):
+    for c in (swap_ids, swap_tok, *far_weights):
         c.start()
 
     @pl.when(chip + 1 < chips)
@@ -304,24 +316,23 @@
         local[n].wait()
     strengths(rows_of(core))
     turns(core)
-    swap_ids.wait()
-
-    @pl.when(chip >= 1)
-    def _():
-        next_same.wait_recv()
-        next_other.wait_recv()
-
-    maps([(core, 0, 0), (core, 0, 1)])
+
+    def ids_arrived():
+        swap_ids.wait()
+
+        @pl.when(chip >= 1)
+        def _():
+            next_same.wait_recv()
+            next_other.wait_recv()
+
+    maps([(core, h, j) for h in range(HERE) for j in range(2)], ids_arrived)
     turns(other)
     swap_tok.wait()
     project(rows_of(other), 0)
+    project(rows_of(other), 1)
     strengths(rows_of(other))
-    maps([(other, 0, 0), (other, 0, 1)])
+    maps([(other, h, j) for h in range(HERE) for j in range(2)])
     send_maps(0)
-    for n in (K1, V1):
-        local[n].wait()
-    project(slice(None), 1)
-    maps([(0, 1, 0), (0, 1, 1), (1, 1, 0), (1, 1, 1)])
     send_maps(1)
 
     local[Q].wait()
@@ -346,13 +357,21 @@
             if b > 0:
                 both = mm3(thr, pre[b])
                 thr, loc = both[:, :128], both[:, 128:] + loc
-            thr_s[h, pl.ds(b * BLK, BLK), :] = jnp.concatenate([thr, loc], axis=1)
+            hi, low = halves(thr)
+            thr_s[h, 0, pl.ds(b * BLK, BLK), :] = hi
+            thr_s[h, 1, pl.ds(b * BLK, BLK), :] = low
+            loc_s[h, pl.ds(b * BLK, BLK), :] = loc
         return carry
 
     lax.fori_loop(0, HERE, local_out, 0)
     local[O].wait()
-    far_weights.wait()
-    pass_weights.start()
+
+    def share(n):
+        far_weights[n].wait()
+        pass_weights[n].start()
+
+    for n in range(3):
+        share(n)
 
     states = []
     for h in range(HERE):
@@ -362,14 +381,17 @@
                 exchange(h, step).wait_recv()
         state = wrecv_s[h].astype(F32)
         for step in (3, 2, 1):
-            state = mm3(recv_s[step - 1, h, :, 0:128].astype(F32), state) + recv_s[step - 1, h, :, 128:256].astype(F32)
+            lift = recv_s[step - 1, h, :, 0:128]
+            state = dot(
+                jnp.concatenate([lift, lift], axis=1), jnp.concatenate(halves(state), axis=0)
+            ) + recv_s[step - 1, h, :, 128:256].astype(F32)
         states.append(halves(state))
 
     def outputs(half):
         done = []
         for h in range(HERE):
-            both = thr_s[h, rows_of(half), :]
-            o = both[:, 128:] + joined(halves(both[:, :128]), states[h])
+            rows = rows_of(half)
+            o = loc_s[h, rows, :] + joined((thr_s[h, 0, rows, :], thr_s[h, 1, rows, :]), states[h])
             o = o * lax.rsqrt(jnp.mean(o * o, axis=-1, keepdims=True) + norm_eps)
             g = gain[:, pl.ds(pl.multiple_of(core * 256 + h * 128, 128), 128)]
             done.append((o * g).astype(BF16))
@@ -390,24 +412,24 @@
         rows = pl.ds(pl.multiple_of(lax.rem(head + step + nhead, nhead) * 64, 64), 64)
         return dot(hid2_s[0, rows, :], wo_s[0:256, cols]) + dot(hid2_s[1, rows, :], wo_s[256:512, cols])
 
-    parts = [slice(n * 512, (n + 1) * 512) for n in range(4)]
-
     def hop(d, n):
         return remote(rs_s.at[d, n], rr_s.at[d, n], rsend.at[d, n], rrecv.at[d, n], along(1 if d == 0 else -1))
 
-    for n, cols in enumerate(parts):
+    for n, cols in enumerate(PARTS):
         for d in range(2):
             rs_s[d, n] = term(1 if d == 0 else -1, cols).astype(BF16)
             hop(d, n).start()
-    sums = [term(0, cols).astype(BF16).astype(F32) for cols in parts]
-    pass_weights.wait()
+    share(3)
+    sums = [term(0, cols).astype(BF16).astype(F32) for cols in PARTS]
+    for c in pass_weights:
+        c.wait()
     far_other.wait()
     far_same.wait()
     far = [far_s[0], far_s[1]]
-    for n, cols in enumerate(parts):
+    for n, cols in enumerate(FETCHED):
         extra = dot(far[0], wf_s[0:256, cols]) + dot(far[1], wf_s[256:512, cols])
         sums[n] = sums[n] + extra.astype(BF16).astype(F32)
-    for n, cols in enumerate(parts):
+    for n, cols in enumerate(PARTS):
         for d in range(2):
             hop(d, n).wait()
             sums[n] = sums[n] + rr_s[d, n].astype(F32)
@@ -441,13 +463,13 @@
             V((2, 2, 128, 128), F32), V((2, 2, 128, 256), F32), V((2, 2, 256, 256), F32), V((2, 2, 16, 256), F32), V((128, 2048), BF16),
             V((16, 8, 128), F32), V((128, 2048), F32), V((16, 8, 128), F32),
             V((2, 2, 2, 2, 256, 256), BF16), V((2, 2, 2, 2, 128, 256), BF16), V((2, 2, 2, 128, 256), F32),
-            V((2, 2, 128, 256), F32), V((2, 512, 256), F32),
+            V((2, 2, 128, 256), F32), V((2, 2, 512, 128), BF16), V((2, 512, 128), F32),
             V((2, 128, 256), BF16), V((3, 2, 128, 256), BF16), V((2, 128, 128), BF16),
             V((256, 256), BF16), V((2, 256, 256), BF16),
             V((2, 64, 256), BF16), V((512, D), BF16), V((2, 4, 64, 512), BF16), V((2, 4, 64, 512), BF16),
             *[
                 pltpu.SemaphoreType.DMA(shape)
-                for shape in ((9,), (2,), (6,), (4, 2), (4, 2), (2,), (4,), (4,), (2, 4), (2, 4))
+                for shape in ((9,), (2,), (6,), (4, 2), (4, 2), (2,), (4,), (4, 4), (2, 4), (2, 4))
             ],
         ],
         compiler_params=pltpu.CompilerParams(

time: 44.6 us -> 41.7 us (0.935)
  Pallas kernels: 42.7 us -> 39.9 us
    pallas_call x1, Pallas kernels: 42.7 us -> 39.9 us  [body(): pl.pallas_call(kernel, out_shape=jax.ShapeDtypeStruct((64, 2048), BF16),...]
where the time goes in v3:
time: 41.7 us; the launch traced here: 41.6 us
  Pallas kernels  39.9 us (96%)
  local copies, waits for them, and re-layouts  1.67 us (4%)
    pallas_call x1, Pallas kernels, body(): pl.pallas_call(kernel, out_shape=jax.ShapeDtypeStruct((64, 2048), BF16),...  39.9 us
    unnamed x1, local copies, waits for them, and re-layouts  1.67 us

profile of v3, /device:TPU:1, one launch (start us, length us, event | category | flops | bytes accessed | tf_op | source)
XLA Modules:
  0.0 41.6 jit_solution(4070318728924866301)
XLA Ops:
  0.0 39.9 %shard_map.91 = bf16[64,2048]{1,0:T(8,128)(2,1)} custom-call(bf16[256,2048]{1,0:T(8,128)(2,1)} %tok.1, s32[2,128]{1,0:T(2,128)} %bitcast.6, bf16[2048,512]{1,0:T(8,128)(2,1)} %qw.1, bf16[2048,1024]{1,0:T(8,128)(2,1)} %kw.1, bf16[2048,1024]{1,0:T(8,128)(2,1)} %vw.1, bf16[8,2048]{1,0:T(8,128)(2,1)} %bitcast.4, f32[1,8]{1,0:T(1,128)} %bitcast.7, ...), custom_call_target="tpu_custom_call" | custom-call | flops 5000000000 | bytes 14000000 | tf_op jit(solution)/shard_map/pallas_call | solution.py:454
  39.9 1.7 %copy.11 = bf16[64,2048]{1,0:T(8,128)(2,1)} copy(bf16[64,2048]{1,0:T(8,128)(2,1)} %shard_map.91) | data formatting | bytes 524288

commit v4 on v3

--- a/solution.py
+++ b/solution.py
@@ -115,7 +115,11 @@
             pl.semaphore_signal(barrier, inc=1, device_id=at(-step, core), device_id_type=MESH)
             if step == 1:
                 pl.semaphore_signal(barrier, inc=1, device_id=at(-step, other), device_id_type=MESH)
-    greeted = len(mutual) + jnp.minimum(chips - 1 - chip, REACH) + jnp.minimum(chips - 1 - chip, 1)
+    @pl.when(lax.rem(chip, 2) == 0)
+    def _():
+        pl.semaphore_signal(barrier, inc=1, device_id=at(1, core), device_id_type=MESH)
+
+    greeted = len(mutual) + lax.rem(chip, 2) + jnp.minimum(chips - 1 - chip, REACH) + jnp.minimum(chips - 1 - chip, 1)
 
     def remote(src, dst, ssem, rsem, peer):
         return pltpu.make_async_remote_copy(
@@ -128,8 +132,16 @@
     half_rows = pl.ds(pl.multiple_of(core * 256, 256), 256)
     far_weights = [
         remote(ow.at[half_rows, cols], wf_s.at[half_rows, cols], wsem.at[0, n], wsem.at[1, n], along(2))
-        for n, cols in enumerate(FETCHED)
+        for n, cols in enumerate(FETCHED[:3])
     ]
+    odd = lax.rem(chip, 2)
+    quarter = pl.ds(pl.multiple_of(core * 256 + odd * 128, 128), 128)
+    far_weights.append(
+        remote(ow.at[quarter, PARTS[3]], wf_s.at[quarter, PARTS[3]], wsem.at[0, 3], wsem.at[1, 3], along(2))
+    )
+    swap_weights = remote(
+        wf_s.at[quarter, PARTS[3]], wf_s.at[quarter, PARTS[3]], wsem.at[4, 0], wsem.at[5, 0], at(1 - 2 * odd, core)
+    )
     pass_weights = [
         remote(wf_s.at[half_rows, cols], wf_s.at[half_rows, cols], wsem.at[2, n], wsem.at[3, n], at(0, other))
         for n, cols in enumerate(FETCHED)
@@ -294,7 +306,7 @@
         local[n].wait()
     project(rows_of(core), 1)
     pl.semaphore_wait(barrier, greeted)
-    for c in (swap_ids, swap_tok, *far_weights):
+    for c in (swap_ids, swap_tok, far_weights[3], *far_weights[:3]):
         c.start()
 
     @pl.when(chip + 1 < chips)
@@ -330,6 +342,8 @@
     swap_tok.wait()
     project(rows_of(other), 0)
     project(rows_of(other), 1)
+    far_weights[3].wait()
+    swap_weights.start()
     strengths(rows_of(other))
     maps([(other, h, j) for h in range(HERE) for j in range(2)])
     send_maps(0)
@@ -370,7 +384,9 @@
         far_weights[n].wait()
         pass_weights[n].start()
 
-    for n in range(3):
+    swap_weights.wait()
+    pass_weights[3].start()
+    for n in range(2):
         share(n)
 
     states = []
@@ -419,7 +435,7 @@
         for d in range(2):
             rs_s[d, n] = term(1 if d == 0 else -1, cols).astype(BF16)
             hop(d, n).start()
-    share(3)
+    share(2)
     sums = [term(0, cols).astype(BF16).astype(F32) for cols in PARTS]
     for c in pass_weights:
         c.wait()
@@ -469,7 +485,7 @@
             V((2, 64, 256), BF16), V((512, D), BF16), V((2, 4, 64, 512), BF16), V((2, 4, 64, 512), BF16),
             *[
                 pltpu.SemaphoreType.DMA(shape)
-                for shape in ((9,), (2,), (6,), (4, 2), (4, 2), (2,), (4,), (4, 4), (2, 4), (2, 4))
+                for shape in ((9,), (2,), (6,), (4, 2), (4, 2), (2,), (4,), (6, 4), (2, 4), (2, 4))
             ],
         ],
         compiler_params=pltpu.CompilerParams(

time: 41.7 us -> 40.3 us (0.966)
  the two profiles are of different devices: /device:TPU:1 before, /device:TPU:97 now
where the time goes in v4:
time: 40.3 us; the launch traced here: 40.1 us
  Pallas kernels  38.4 us (95%)
  local copies, waits for them, and re-layouts  1.67 us (4%)
    pallas_call x1, Pallas kernels, body(): pl.pallas_call(kernel, out_shape=jax.ShapeDtypeStruct((64, 2048), BF16),...  38.4 us
    unnamed x1, local copies, waits for them, and re-layouts  1.67 us

profile of v4, /device:TPU:97, one launch (start us, length us, event | category | flops | bytes accessed | tf_op | source)
XLA Modules:
  0.0 40.1 jit_solution(13709991215060144655)
XLA Ops:
  0.0 38.4 %shard_map.91 = bf16[64,2048]{1,0:T(8,128)(2,1)} custom-call(bf16[256,2048]{1,0:T(8,128)(2,1)} %tok.1, s32[2,128]{1,0:T(2,128)} %bitcast.6, bf16[2048,512]{1,0:T(8,128)(2,1)} %qw.1, bf16[2048,1024]{1,0:T(8,128)(2,1)} %kw.1, bf16[2048,1024]{1,0:T(8,128)(2,1)} %vw.1, bf16[8,2048]{1,0:T(8,128)(2,1)} %bitcast.4, f32[1,8]{1,0:T(1,128)} %bitcast.7, ...), custom_call_target="tpu_custom_call" | custom-call | flops 5000000000 | bytes 14000000 | tf_op jit(solution)/shard_map/pallas_call | solution.py:470
  38.4 1.7 %copy.11 = bf16[64,2048]{1,0:T(8,128)(2,1)} copy(bf16[64,2048]{1,0:T(8,128)(2,1)} %shard_map.91) | data formatting | bytes 524288
